TPU v7x, 32 devices: a whole 2x2x4 slice. The times are simulated.
32 devices in a mesh: blk: 8 (over z, x), blade: 4 (over y, core).
Axes of the slice: x: 2, y: 2, z: 4, core: 2. Of those that a mesh axis runs over, the one named last changes fastest.
Arguments:
- bnd_pos: float32 [3, 2048], P(None, 'blk'), may hold values from -1 to 1
- bnd_owner: int32 [2048, 1], P('blk'), may hold values from 0 to 7; in each aligned block of 256 rows (0 to 255, 256 to 511, ...) at most 64 rows name the same one
- bnd_slot: int32 [2048], P('blk'), may hold values from 0 to 16383
- seg_start: float32 [3, 4, 1024], P(None, 'blade', 'blk'), may hold values from -1 to 1
- seg_step: float32 [3, 4, 1024], P(None, 'blade', 'blk'), may hold values from -0.15 to 0.15
- seg_gamma: float32 [4, 1024], P('blade', 'blk'), may hold values from -6 to 6
- seg_sec: int32 [4, 1024], P('blade', 'blk'), may hold values from 0 to 63
- flow: float32 [3, 64, 64, 256], P(None, 'blk', 'blade'), may hold values from -6 to 6
- source: float32 [3, 64, 64, 256], P(None, 'blk', 'blade'), may hold values from -6 to 6
- extra_diag: float32 [64, 64, 256], P('blk', 'blade'), may hold values from 0.25 to 2
- circ_weight: float32 [64, 64, 256], P('blk', 'blade'), may hold values from -0.125 to 0.125
- sec_block: int32 [4, 64], replicated, may hold values from 0 to 7
- sec_row: int32 [4, 64], replicated, may hold values from 0 to 15
Outputs:
- new_flow: float32 [3, 64, 64, 256], P(None, 'blk', 'blade')
- new_gamma: float32 [4, 1024], P('blade', 'blk')
Inputs may be any that keep to these rules, and one draw needn't show every extreme that they name: `bnd_owner`: among the 256 boundary cells of each aligned block (one index of blk), at most 64 have the same owner, and some owner has exactly 64.
All inputs are finite; a program needn't handle non-finite values.
Results may differ from a plain program's by a relative error of at most 0.0001.
Values sent between devices are 32-bit elements; how exact they have to be, the bound alone decides.
A program may use at most 64 MiB of HBM per device.

v0:
```python
import math

import jax
import jax.numpy as jnp
from jax import lax
from jax.sharding import PartitionSpec as P

PASSES = 2


CORE = 0.01
FOUR_PI = 4.0 * math.pi
OMEGA = 0.8
RELAX = 0.5


def with_halo(array, sides, width):
    for axis, dim in sides:
        size, length = (lax.axis_size(axis), array.shape[dim])
        up = [(i, (i + 1) % size) for i in range(size - 1)]
        down = [(j, i) for i, j in up]
        last = lax.slice_in_dim(array, length - width, length, axis=dim)
        leading = lax.slice_in_dim(array, 0, width, axis=dim)
        before = lax.ppermute(last, axis, up)
        after = lax.ppermute(leading, axis, down)
        array = jnp.concatenate([before, array, after], axis=dim)
    return array


def pair_velocity(points, segs):
    p = points[:, :, None]
    start = segs[0:3, None, :]
    step = segs[3:6, None, :]
    gamma = segs[6][None, :]
    r1 = p - start
    r2 = r1 - step
    cross_x = r1[1] * r2[2] - r1[2] * r2[1]
    cross_y = r1[2] * r2[0] - r1[0] * r2[2]
    cross_z = r1[0] * r2[1] - r1[1] * r2[0]
    cross_sq = cross_x * cross_x + cross_y * cross_y + cross_z * cross_z
    norm_one = jnp.sqrt(jnp.sum(r1 * r1, 0) + CORE)
    norm_two = jnp.sqrt(jnp.sum(r2 * r2, 0) + CORE)
    step_sq = jnp.sum(step * step, 0)
    along = jnp.sum(step * (r1 / norm_one - r2 / norm_two), 0)
    weight = gamma * along / (FOUR_PI * (cross_sq + CORE * step_sq + CORE * CORE))
    return jnp.stack(
        [jnp.sum(weight * cross_x, 1), jnp.sum(weight * cross_y, 1), jnp.sum(weight * cross_z, 1)]
    )


def spanned(points, segs, width):
    count = segs.shape[1]
    if count > width and count % width == 0:

        def add_part(index, total):
            part = lax.dynamic_slice_in_dim(segs, index * width, width, 1)
            return total + pair_velocity(points, part)

        return lax.fori_loop(
            0, count // width, add_part, jnp.zeros((3, points.shape[1]), jnp.float32)
        )
    return pair_velocity(points, segs)


def sweep(padded, rhs, dgl):
    zpad = jnp.pad(padded, ((0, 0), (0, 0), (0, 0), (1, 1)))
    center = padded[:, 1:-1, 1:-1, :]
    beside = zpad[:, 2:, 1:-1, 1:-1] + zpad[:, :-2, 1:-1, 1:-1]
    beside = beside + zpad[:, 1:-1, 2:, 1:-1] + zpad[:, 1:-1, :-2, 1:-1]
    beside = beside + zpad[:, 1:-1, 1:-1, 2:] + zpad[:, 1:-1, 1:-1, :-2]
    resid = rhs - (dgl * center - beside)
    return center + OMEGA * resid / dgl


def per_device(
    bnd_pos,
    bnd_owner,
    bnd_slot,
    seg_start,
    seg_step,
    seg_gamma,
    seg_sec,
    flow,
    source,
    extra_diag,
    circ_weight,
    sec_block,
    sec_row,
):
    n_blk = lax.axis_size("blk")
    cells = bnd_pos.shape[1]
    cap = max(2, 2 * cells // n_blk)
    depth_y = flow.shape[2]
    depth_z = flow.shape[3]
    own_wake = jnp.concatenate([seg_start[:, 0], seg_step[:, 0], seg_gamma], 0)
    partial_value = spanned(bnd_pos, lax.all_gather(own_wake, "blk", axis=1, tiled=True), 2048)
    velocity = lax.psum(partial_value, "blade")
    owner = bnd_owner[:, 0]
    onehot = (owner[:, None] == jnp.arange(n_blk, dtype=jnp.int32)[None, :]).astype(jnp.int32)
    rank = jnp.sum(jnp.cumsum(onehot, 0) * onehot, 1) - 1
    where_to = owner * cap + rank
    payload = jnp.concatenate([velocity, bnd_slot.astype(jnp.float32)[None]], 0)
    outgoing = (
        jnp.zeros((4, n_blk * cap), jnp.float32).at[:, where_to].set(payload).reshape(4, n_blk, cap)
    )
    incoming = lax.all_to_all(outgoing, "blk", split_axis=1, concat_axis=1, tiled=True).reshape(
        4, n_blk * cap
    )
    slot = incoming[3].astype(jnp.int32)
    blade_index = lax.axis_index("blade")
    local_y = slot // depth_z - blade_index * depth_y
    local_z = slot % depth_z
    keep = (local_y >= 0) & (local_y < depth_y)
    values = jnp.where(keep[None, :], incoming[:3], 0.0)
    face = (
        jnp.zeros((3, depth_y, depth_z), jnp.float32)
        .at[:, jnp.clip(local_y, 0, depth_y - 1), local_z]
        .add(values)
    )
    rhs = source.at[:, 0].add(face)
    dgl = 6.0 + extra_diag
    state = flow
    for step in range(PASSES):
        padded = with_halo(state, (("blk", 1), ("blade", 2)), 1)
        state = sweep(padded, rhs, dgl)
    profile = jnp.sum(circ_weight * state[1], axis=(0, 2))
    profiles = lax.all_gather(profile[None], "blk", axis=0, tiled=True)
    block_row = lax.dynamic_index_in_dim(sec_block, blade_index, 0, keepdims=False)
    row_here = lax.dynamic_index_in_dim(sec_row, blade_index, 0, keepdims=False)
    section = profiles[block_row, row_here]
    nsec = section.shape[0]
    match = seg_sec[0][:, None] == jnp.arange(nsec, dtype=jnp.int32)[None, :]
    looked = jnp.sum(jnp.where(match, section[None, :], 0.0), 1)
    new_gamma = ((1.0 - RELAX) * seg_gamma[0] + RELAX * looked)[None]
    return (state, new_gamma)


def solution(mesh):
    return jax.shard_map(
        per_device,
        mesh=mesh,
        in_specs=(
            P(None, "blk"),
            P("blk", None),
            P("blk"),
            P(None, "blade", "blk"),
            P(None, "blade", "blk"),
            P("blade", "blk"),
            P("blade", "blk"),
            P(None, "blk", "blade", None),
            P(None, "blk", "blade", None),
            P("blk", "blade", None),
            P("blk", "blade", None),
            P(),
            P(),
        ),
        out_specs=(P(None, "blk", "blade", None), P("blade", "blk")),
        check_vma=False,
    )
```

profile of v0, /device:TPU:0, one launch (start us, length us, event | category | flops | bytes accessed | tf_op | source)
XLA Modules:
  0.0 135.2 jit_solution(2110822875356458950)
XLA Ops:
  0.6 0.7 copy_bitcast_fusion
  2.0 32.2 %all_gather.6 = f32[7,1024]{1,0:T(8,128)S(1)} all-gather(f32[7,128]{1,0:T(8,128)S(1)} %pad_maximum_fusion.15), channel_id=1, replica_groups=mesh['blk'=8,'blade'=4] {'blk'}, dimensions={1}, use_global_device_ids=true | all-gather | bytes 32256 | tf_op jit(solution)/shard_map/all_gather | solution.py:96
  34.2 1.7 %fusion.2 = (f32[256,1024]{1,0:T(8,128)S(1)}, f32[256,1024]{1,0:T(8,128)S(1)}, f32[3,256,1024]{2,1,0:T(8,128)S(1)}) fusion(f32[3,1024]{1,0:T(4,128)S(1)} %get-tuple-element.34, f32[3,256]{1,0:T(4,128)} %param.15, f32[3,1024]{1,0:T(4,128)S(1)} %get-tuple-element.35), kind=kLoop, calls=%fused_computation.8 | loop fusion | flops 4194304 | bytes 5270528 | tf_op jit(solution)/shard_map/reduce_sum | solution.py:41
  36.9 0.9 subtract_subtract_fusion
  37.7 1.4 %fusion.9 = (f32[256,1024]{1,0:T(8,128)S(1)}, f32[1,256,1024]{2,1,0:T(8,128)S(1)}, f32[1,256,1024]{2,1,0:T(8,128)S(1)}, f32[1,256,1024]{2,1,0:T(8,128)S(1)}) fusion(f32[256,1024]{1,0:T(8,128)S(1)} %get-tuple-element.32, f32[1024]{0:T(1024)S(1)} %broadcast_multiply_fusion, f32[1024]{0:T(1024)S(1)} %bitcast.96, f32[3,256,1024]{2,1,0:T(8,128)S(1)} %get-tuple-element.31, ...), kind=kLoop, calls=%fused_computation.27 | loop fusion | flops 4980736 | bytes 11542528 | tf_op jit(solution)/shard_map/div | solution.py:45
  39.5 5.7 %psum.7 = f32[3,256]{1,0:T(4,128)S(1)} all-reduce(f32[3,256]{1,0:T(4,128)S(1)} %pad_maximum_fusion.16), channel_id=1, replica_groups=mesh['blk'=8,'blade'=4] {'blade'}, use_global_device_ids=true, to_apply=%region_10.11 | all-reduce | flops 768 | bytes 6144 | tf_op jit(solution)/shard_map/psum | solution.py:97
  46.3 1.2 scatter_custom_fusion
  47.7 0.7 reshape.330
  48.4 5.5 %all-to-all-start = ((f32[8,1,256]{2,1,0:T(1,128)}), f32[8,1,256]{2,1,0:T(1,128)S(1)}, u32[]{:S(2)}, u32[]{:S(2)}) async-start(f32[8,1,256]{2,1,0:T(1,128)} %reshape.330), calls=%async_computation | async-start | bytes 16384 | tf_op jit(solution)/shard_map/all_to_all | solution.py:106
  53.9 3.9 %collective-permute-start.1 = (f32[3,1,16,256]{3,2,1,0:T(8,128)S(1)}, f32[3,1,16,256]{3,2,1,0:T(8,128)S(1)}, u32[]{:S(2)}, u32[]{:S(2)}) collective-permute-start(f32[3,1,16,256]{3,2,1,0:T(8,128)S(1)} %get-tuple-element.30), channel_id=1, source_target_pairs={{0,4},{4,8},{8,12},{12,16},{16,20},{20,24},{24,28},{1,5},{5,9},{9,... | collective-permute-start | bytes 147464 | tf_op jit(solution)/shard_map/ppermute | solution.py:24
  57.8 1.3 collective-permute-start
  59.1 1.2 all-to-all-done
  62.4 24.6 %scatter_fusion = f32[3,16,256]{0,2,1:T(8,128)S(1)} fusion(f32[3,16,256]{0,2,1:T(8,128)S(1)} %broadcast_in_dim.28, s32[512]{0:T(512)S(1)} %bitcast.90, f32[512,3]{1,0:T(8,128)S(1)} %copy.41), kind=kCustom, calls=%fused_computation.2 | custom fusion | flops 1536 | bytes 22528 | tf_op jit(solution)/shard_map/scatter-add | solution.py:118
  87.7 1.3 collective-permute-start.2
  89.0 3.0 %collective-permute-start.3 = (f32[3,10,1,256]{3,2,1,0:T(1,128)S(1)}, f32[3,10,1,256]{3,2,1,0:T(1,128)S(1)}, u32[]{:S(2)}, u32[]{:S(2)}) collective-permute-start(f32[3,10,1,256]{3,2,1,0:T(1,128)S(1)} %get-tuple-element.25), channel_id=1, source_target_pairs={{0,1},{1,2},{2,3},{4,5},{5,6},{6,7},{8,9},{9,10},{10,11},{12,13},{... | collective-permute-start | bytes 92168 | tf_op jit(solution)/shard_map/ppermute | solution.py:24
  92.1 0.8 collective-permute-done.3
  93.9 1.3 collective-permute-start.4
  95.2 4.5 %collective-permute-start.5 = (f32[3,1,16,256]{3,2,1,0:T(8,128)S(1)}, f32[3,1,16,256]{3,2,1,0:T(8,128)S(1)}, u32[]{:S(2)}, u32[]{:S(2)}) collective-permute-start(f32[3,1,16,256]{3,2,1,0:T(8,128)S(1)} %get-tuple-element.27), channel_id=1, source_target_pairs={{0,4},{4,8},{8,12},{12,16},{16,20},{20,24},{24,28},{1,5},{5,9},{9,... | collective-permute-start | bytes 147464 | tf_op jit(solution)/shard_map/ppermute | solution.py:24
  99.9 1.6 %collective-permute-done.5 = f32[3,1,16,256]{3,2,1,0:T(8,128)S(1)} collective-permute-done((f32[3,1,16,256]{3,2,1,0:T(8,128)S(1)}, f32[3,1,16,256]{3,2,1,0:T(8,128)S(1)}, u32[]{:S(2)}, u32[]{:S(2)}) %collective-permute-start.5) | collective-permute-done | bytes 49184 | tf_op jit(solution)/shard_map/ppermute | solution.py:24
  101.6 1.3 collective-permute-start.6
  102.9 3.2 %collective-permute-start.7 = (f32[3,10,1,256]{3,2,1,0:T(1,128)S(1)}, f32[3,10,1,256]{3,2,1,0:T(1,128)S(1)}, u32[]{:S(2)}, u32[]{:S(2)}) collective-permute-start(f32[3,10,1,256]{3,2,1,0:T(1,128)S(1)} %get-tuple-element.23), channel_id=1, source_target_pairs={{0,1},{1,2},{2,3},{4,5},{5,6},{6,7},{8,9},{9,10},{10,11},{12,13},{... | collective-permute-start | bytes 92168 | tf_op jit(solution)/shard_map/ppermute | solution.py:24
  106.0 0.7 or_bitcast_fusion
  109.9 23.8 %all-reduce.2 = f32[128]{0:T(128)S(1)} all-reduce(f32[128]{0:T(128)S(1)} %dynamic-update-slice.3), channel_id=2, replica_groups=mesh['blk'=8,'blade'=4] {'blk'}, use_global_device_ids=true, to_apply=%add.2 | all-reduce | flops 128 | bytes 1024
  133.8 0.7 gather_fusion
  (83 shorter events, 10.2 us)
Async XLA Ops:
  36.2 0.7 copy-start.5
  39.1 6.1 %copy-start.7 = (s32[256]{0:T(256)S(1)}, s32[256]{0:T(256)}, u32[]{:S(2)}) copy-start(s32[256]{0:T(256)} %param.17) | copy-start | bytes 3076
  39.1 6.2 %copy-start.6 = (s32[256,1]{0,1:T(1,128)S(1)}, s32[256,1]{0,1:T(1,128)}, u32[]{:S(2)}) copy-start(s32[256,1]{0,1:T(1,128)} %param.16) | copy-start | bytes 3076
  39.1 14.7 %copy-start.1 = (f32[3,8,16,256]{3,2,1,0:T(8,128)S(1)}, f32[3,8,16,256]{3,2,1,0:T(8,128)}, u32[]{:S(2)}) copy-start(f32[3,8,16,256]{3,2,1,0:T(8,128)} %param.22) | copy-start | bytes 1179652
  39.5 19.6 %copy-start.3 = (f32[8,16,256]{2,1,0:T(8,128)S(1)}, f32[8,16,256]{2,1,0:T(8,128)}, u32[]{:S(2)}) copy-start(f32[8,16,256]{2,1,0:T(8,128)} %param.24) | copy-start | bytes 393220
  48.4 12.0 %all-to-all-start = ((f32[8,1,256]{2,1,0:T(1,128)}), f32[8,1,256]{2,1,0:T(1,128)S(1)}, u32[]{:S(2)}, u32[]{:S(2)}) async-start(f32[8,1,256]{2,1,0:T(1,128)} %reshape.330), calls=%async_computation | async-start | bytes 16384 | tf_op jit(solution)/shard_map/all_to_all | solution.py:106
  53.9 33.7 %collective-permute-start.1 = (f32[3,1,16,256]{3,2,1,0:T(8,128)S(1)}, f32[3,1,16,256]{3,2,1,0:T(8,128)S(1)}, u32[]{:S(2)}, u32[]{:S(2)}) collective-permute-start(f32[3,1,16,256]{3,2,1,0:T(8,128)S(1)} %get-tuple-element.30), channel_id=1, source_target_pairs={{0,4},{4,8},{8,12},{12,16},{16,20},{20,24},{24,28},{1,5},{5,9},{9,... | collective-permute-start | bytes 147464 | tf_op jit(solution)/shard_map/ppermute | solution.py:24
  57.8 29.9 %collective-permute-start = (f32[3,1,16,256]{3,2,1,0:T(8,128)S(1)}, f32[3,1,16,256]{3,2,1,0:T(8,128)S(1)}, u32[]{:S(2)}, u32[]{:S(2)}) collective-permute-start(f32[3,1,16,256]{3,2,1,0:T(8,128)S(1)} %get-tuple-element.29), channel_id=1, source_target_pairs={{4,0},{8,4},{12,8},{16,12},{20,16},{24,20},{28,24},{5,1},{9,5},{13... | collective-permute-start | bytes 147464 | tf_op jit(solution)/shard_map/ppermute | solution.py:25
  87.0 5.1 %copy-start = (f32[3,8,16,256]{3,2,1,0:T(8,128)S(1)}, f32[3,8,16,256]{3,2,1,0:T(8,128)}, u32[]{:S(2)}) copy-start(f32[3,8,16,256]{3,2,1,0:T(8,128)} %param.23) | copy-start | bytes 1179652
  87.7 4.4 %collective-permute-start.2 = (f32[3,10,1,256]{3,2,1,0:T(1,128)S(1)}, f32[3,10,1,256]{3,2,1,0:T(1,128)S(1)}, u32[]{:S(2)}, u32[]{:S(2)}) collective-permute-start(f32[3,10,1,256]{3,2,1,0:T(1,128)S(1)} %get-tuple-element.26), channel_id=1, source_target_pairs={{1,0},{2,1},{3,2},{5,4},{6,5},{7,6},{9,8},{10,9},{11,10},{13,12},{... | collective-permute-start | bytes 92168 | tf_op jit(solution)/shard_map/ppermute | solution.py:25
  89.0 3.9 %collective-permute-start.3 = (f32[3,10,1,256]{3,2,1,0:T(1,128)S(1)}, f32[3,10,1,256]{3,2,1,0:T(1,128)S(1)}, u32[]{:S(2)}, u32[]{:S(2)}) collective-permute-start(f32[3,10,1,256]{3,2,1,0:T(1,128)S(1)} %get-tuple-element.25), channel_id=1, source_target_pairs={{0,1},{1,2},{2,3},{4,5},{5,6},{6,7},{8,9},{9,10},{10,11},{12,13},{... | collective-permute-start | bytes 92168 | tf_op jit(solution)/shard_map/ppermute | solution.py:24
  93.5 13.2 %copy-start.10 = (u32[32]{0:T(128)S(1)}, u32[32]{0:T(128)}, u32[]{:S(2)}) copy-start(u32[32]{0:T(128)} %constant.144) | copy-start | bytes 388
  93.9 6.0 %collective-permute-start.4 = (f32[3,1,16,256]{3,2,1,0:T(8,128)S(1)}, f32[3,1,16,256]{3,2,1,0:T(8,128)S(1)}, u32[]{:S(2)}, u32[]{:S(2)}) collective-permute-start(f32[3,1,16,256]{3,2,1,0:T(8,128)S(1)} %get-tuple-element.28), channel_id=1, source_target_pairs={{4,0},{8,4},{12,8},{16,12},{20,16},{24,20},{28,24},{5,1},{9,5},{13... | collective-permute-start | bytes 147464 | tf_op jit(solution)/shard_map/ppermute | solution.py:25
  95.2 6.3 %collective-permute-start.5 = (f32[3,1,16,256]{3,2,1,0:T(8,128)S(1)}, f32[3,1,16,256]{3,2,1,0:T(8,128)S(1)}, u32[]{:S(2)}, u32[]{:S(2)}) collective-permute-start(f32[3,1,16,256]{3,2,1,0:T(8,128)S(1)} %get-tuple-element.27), channel_id=1, source_target_pairs={{0,4},{4,8},{8,12},{12,16},{16,20},{20,24},{24,28},{1,5},{5,9},{9,... | collective-permute-start | bytes 147464 | tf_op jit(solution)/shard_map/ppermute | solution.py:24
  101.6 6.4 %collective-permute-start.6 = (f32[3,10,1,256]{3,2,1,0:T(1,128)S(1)}, f32[3,10,1,256]{3,2,1,0:T(1,128)S(1)}, u32[]{:S(2)}, u32[]{:S(2)}) collective-permute-start(f32[3,10,1,256]{3,2,1,0:T(1,128)S(1)} %get-tuple-element.24), channel_id=1, source_target_pairs={{1,0},{2,1},{3,2},{5,4},{6,5},{7,6},{9,8},{10,9},{11,10},{13,12},{... | collective-permute-start | bytes 92168 | tf_op jit(solution)/shard_map/ppermute | solution.py:25
  102.9 5.1 %collective-permute-start.7 = (f32[3,10,1,256]{3,2,1,0:T(1,128)S(1)}, f32[3,10,1,256]{3,2,1,0:T(1,128)S(1)}, u32[]{:S(2)}, u32[]{:S(2)}) collective-permute-start(f32[3,10,1,256]{3,2,1,0:T(1,128)S(1)} %get-tuple-element.23), channel_id=1, source_target_pairs={{0,1},{1,2},{2,3},{4,5},{5,6},{6,7},{8,9},{9,10},{10,11},{12,13},{... | collective-permute-start | bytes 92168 | tf_op jit(solution)/shard_map/ppermute | solution.py:24
  108.6 0.9 copy-start.4
  108.6 25.9 %copy-start.9 = (s32[1,128]{1,0:T(1,128)S(1)}, s32[1,128]{1,0:T(1,128)}, u32[]{:S(2)}) copy-start(s32[1,128]{1,0:T(1,128)} %param.21) | copy-start | bytes 1540
  108.6 26.0 %copy-start.8 = (f32[1,128]{1,0:T(1,128)S(1)}, f32[1,128]{1,0:T(1,128)}, u32[]{:S(2)}) copy-start(f32[1,128]{1,0:T(1,128)} %param.20) | copy-start | bytes 1540
  109.5 25.6 %copy-start.2 = (f32[3,8,16,256]{3,2,1,0:T(8,128)}, f32[3,8,16,256]{3,2,1,0:T(8,128)S(1)}, u32[]{:S(2)}) copy-start(f32[3,8,16,256]{3,2,1,0:T(8,128)S(1)} %fusion.18) | copy-start | bytes 1179652
where the time goes:
time: 137 us; the launch traced here: 135 us
  blocking collectives  61.7 us (45%)
  other arithmetic  35.1 us (26%)
  starting transfers between devices  25.3 us (18%)
  local copies, waits for them, and re-layouts  7.59 us (6%)
  waiting for transfers between devices  3.77 us (3%)
  between operations  1.77 us (1%)
    all_gather x1, blocking collectives, per_device(): lax.all_gather(own_wake, 'blk', axis=1, tiled=True)  32.2 us
    scatter-add x1, other arithmetic, per_device(): face = jnp.zeros((3, depth_y, depth_z), jnp.float32).at[:, jnp.clip(local...  24.6 us
    unnamed x1, blocking collectives  23.8 us
    ppermute x4, starting transfers between devices, with_halo(): before = lax.ppermute(last, axis, up)  14.7 us
    psum x1, blocking collectives, per_device(): velocity = lax.psum(partial_value, 'blade')  5.67 us
    all_to_all x1, starting transfers between devices, per_device(): lax.all_to_all(outgoing, 'blk', split_axis=1, concat_axis=1, tiled=True)  5.46 us
    ppermute x4, starting transfers between devices, with_halo(): after = lax.ppermute(leading, axis, down)  5.17 us
    unnamed x30, local copies, waits for them, and re-layouts  3.29 us
  transfers between devices with their start and end apart: 9, of which 4 were waited for; matrix products, arithmetic and copies ran while one was open for 21% of the time, Pallas kernels for 0%

commit v1 on v0

v1 whole, which is shorter than its diff:
```python
import functools
import math

import jax
import jax.numpy as jnp
from jax import lax
from jax.experimental import pallas as pl
from jax.experimental.pallas import tpu as pltpu
from jax.sharding import PartitionSpec as P

CORE = 0.01
FOUR_PI = 4.0 * math.pi
OMEGA = 0.8
RELAX = 0.5
LANES = 128
MESH = pl.DeviceIdType.MESH


def kernel(
    n_blk,
    n_bld,
    pos_ref,
    own_ref,
    slot_ref,
    start_ref,
    step_ref,
    gam_ref,
    sec_ref,
    sblk_ref,
    srow_ref,
    flow_ref,
    src_ref,
    diag_ref,
    circ_ref,
    out_ref,
    ng_ref,
    gath,
    vel,
    prof,
    flow_v,
    mid_v,
    out_v,
    src_v,
    diag_v,
    circ_v,
    m_v,
    ysend,
    yrecv,
    dgn_v,
    pos8,
    post,
    pb,
    keys,
    zt,
    lhs,
    sem_in,
    sem_out,
    wake_send,
    wake_recv,
    vel_send,
    vel_recv,
    prof_send,
    prof_recv,
    halo_send,
    halo_recv,
):
    n = n_blk * n_bld
    b = lax.axis_index("blk")
    j = lax.axis_index("blade")
    me = b * n_bld + j
    _, cx, cy, cz = src_v.shape
    half = pb.shape[1]
    n_pair = n // 2
    zbits = cz.bit_length() - 1

    def dev(d):
        return (lax.div(d, n_bld), lax.rem(d, n_bld))

    loads = [
        pltpu.make_async_copy(flow_ref, flow_v.at[:, pl.ds(1, cx)], sem_in.at[0]),
        pltpu.make_async_copy(diag_ref, diag_v, sem_in.at[1]),
        pltpu.make_async_copy(src_ref, src_v, sem_in.at[2]),
        pltpu.make_async_copy(circ_ref, circ_v, sem_in.at[3]),
    ]
    for copy in loads:
        copy.start()

    barrier = pltpu.get_barrier_semaphore()

    @pl.loop(1, n)
    def _(i):
        pl.semaphore_signal(
            barrier, inc=1, device_id=dev(lax.rem(me + i, n)), device_id_type=MESH
        )

    lane1 = lax.broadcasted_iota(jnp.int32, (8, LANES), 1)
    low1 = lane1 < half
    slot_row = jnp.broadcast_to(
        slot_ref[pl.ds(lax.div(j, 2), 1), :].astype(jnp.float32), (8, LANES)
    )
    own_row = jnp.broadcast_to(
        own_ref[pl.ds(lax.div(j, 2), 1), :].astype(jnp.float32), (8, LANES)
    )
    mine_low = lax.rem(j, 2) == 0
    own_row = pltpu.roll(own_row, half, 1)
    first = jnp.where(low1, slot_row, own_row)
    second = jnp.where(low1, own_row, slot_row)
    tag = jnp.where(mine_low, first, second)
    gath[me, 0:3, :] = start_ref[:, 0, :]
    gath[me, 3:6, :] = step_ref[:, 0, :]
    gath[me, 6:7, :] = gam_ref[...]
    gath[me, 7:8, :] = tag[0:1, :]

    pl.semaphore_wait(barrier, n - 1)

    def wake_copy(dst, slot):
        return pltpu.make_async_remote_copy(
            src_ref=gath.at[me],
            dst_ref=gath.at[me],
            send_sem=wake_send.at[slot],
            recv_sem=wake_recv.at[me],
            device_id=dev(dst),
            device_id_type=MESH,
        )

    @pl.loop(1, n)
    def _(i):
        wake_copy(lax.rem(me + i, n), i).start()

    has = (b < n_blk - 1, b > 0, j < n_bld - 1, j > 0)
    nxt_b, prv_b = (b + 1, j), (b - 1, j)
    nxt_j, prv_j = (b, j + 1), (b, j - 1)

    def halo_copies(stage):
        base = 4 * stage
        to_next = flow_ref.at[:, cx - 1] if stage == 0 else mid_v.at[:, cx]
        to_prev = flow_ref.at[:, 0] if stage == 0 else mid_v.at[:, 1]
        grid = flow_v if stage == 0 else mid_v
        pairs = [
            (to_next, grid.at[:, 0], nxt_b, 0),
            (to_prev, grid.at[:, cx + 1], prv_b, 1),
            (ysend.at[stage, 0], yrecv.at[stage, 0], nxt_j, 2),
            (ysend.at[stage, 1], yrecv.at[stage, 1], prv_j, 3),
        ]
        return [
            pltpu.make_async_remote_copy(
                src_ref=s,
                dst_ref=d,
                send_sem=halo_send.at[base + k],
                recv_sem=halo_recv.at[base + k],
                device_id=to,
                device_id_type=MESH,
            )
            for s, d, to, k in pairs
        ]

    def guarded(cond, action):
        @pl.when(cond)
        def _():
            action()

    diag_copy = pltpu.make_async_remote_copy(
        src_ref=diag_ref.at[0],
        dst_ref=dgn_v,
        send_sem=halo_send.at[8],
        recv_sem=halo_recv.at[8],
        device_id=prv_b,
        device_id_type=MESH,
    )
    halo0 = halo_copies(0)
    halo1 = halo_copies(1)
    guarded(has[0], halo0[0].start)
    guarded(has[1], halo0[1].start)

    arrives = (has[1], has[0], has[3], has[2])

    @pl.when(b == 0)
    def _():
        flow_v[:, 0] = jnp.zeros((3, cy, cz), jnp.float32)
        mid_v[:, 0] = jnp.zeros((3, cy, cz), jnp.float32)

    @pl.when(b == n_blk - 1)
    def _():
        flow_v[:, cx + 1] = jnp.zeros((3, cy, cz), jnp.float32)
        mid_v[:, cx + 1] = jnp.zeros((3, cy, cz), jnp.float32)
        dgn_v[...] = jnp.zeros((cy, cz), jnp.float32)

    @pl.when(j == 0)
    def _():
        yrecv[:, 0] = jnp.zeros(yrecv.shape[:1] + yrecv.shape[2:], jnp.float32)

    @pl.when(j == n_bld - 1)
    def _():
        yrecv[:, 1] = jnp.zeros(yrecv.shape[:1] + yrecv.shape[2:], jnp.float32)

    loads[0].wait()
    loads[1].wait()
    for c in range(3):
        ysend[0, 0, c] = flow_v[c, 1 : cx + 1, cy - 1, :]
        ysend[0, 1, c] = flow_v[c, 1 : cx + 1, 0, :]
    ysend[0, 0, 3] = diag_v[:, cy - 1, :]
    ysend[0, 1, 3] = diag_v[:, 0, :]
    guarded(has[2], halo0[2].start)
    guarded(has[3], halo0[3].start)
    guarded(has[1], diag_copy.start)

    pos8[...] = jnp.zeros(pos8.shape, jnp.float32)
    pos8[0:3, :] = pos_ref[...]
    post[...] = pos8[...].T
    mine = post[pl.ds(pl.multiple_of(j * half, half), half), :]
    for c in range(3):
        pb[c] = jnp.broadcast_to(mine[:, c : c + 1], (half, LANES))

    n_sec = sblk_ref.shape[1]
    place = sblk_ref[pl.ds(j, 1), :] * cy + srow_ref[pl.ds(j, 1), :]
    place = jnp.broadcast_to(place.astype(jnp.float32), (n_sec, n_sec))
    eye = lax.broadcasted_iota(jnp.int32, (n_sec, n_sec), 0) == lax.broadcasted_iota(
        jnp.int32, (n_sec, n_sec), 1
    )
    place = jnp.sum(jnp.where(eye, place, 0.0), axis=1, keepdims=True)
    match = lax.broadcasted_iota(jnp.int32, (n_sec, LANES), 0) == sec_ref[...]
    seg_place = jnp.sum(jnp.where(match, place, 0.0), axis=0, keepdims=True)

    row_id = lax.broadcasted_iota(jnp.int32, (cy, cz), 0)
    col_id = lax.broadcasted_iota(jnp.int32, (cy, cz), 1)

    def beside_plane(u, left, right):
        total = jnp.where(row_id == 0, left, pltpu.roll(u, 1, 0))
        total += jnp.where(row_id == cy - 1, right, pltpu.roll(u, cy - 1, 0))
        total += jnp.where(col_id == 0, 0.0, pltpu.roll(u, 1, 1))
        total += jnp.where(col_id == cz - 1, 0.0, pltpu.roll(u, cz - 1, 1))
        return total

    def relaxed(grid, stage, c, x, m):
        u = grid[c, x + 1]
        left = yrecv[stage, 0, c, pl.ds(x, 1), :]
        right = yrecv[stage, 1, c, pl.ds(x, 1), :]
        beside = beside_plane(u, left, right) + grid[c, x] + grid[c, x + 2]
        return (1.0 - OMEGA) * u + m * (src_v[c, x] + beside)

    loads[2].wait()
    for k in range(4):
        guarded(arrives[k], halo0[k].wait_recv)

    @pl.loop(0, cx)
    def _(x):
        m = OMEGA / (6.0 + diag_v[x])
        m_v[x] = m
        for c in range(3):
            mid_v[c, x + 1] = relaxed(flow_v, 0, c, x, m)

    for c in range(3):
        ysend[1, 0, c] = mid_v[c, 1 : cx + 1, cy - 1, :]
        ysend[1, 1, c] = mid_v[c, 1 : cx + 1, 0, :]
    ysend[1, 0, 3] = jnp.zeros((cx, cz), jnp.float32)
    ysend[1, 1, 3] = jnp.zeros((cx, cz), jnp.float32)
    for k in range(4):
        guarded(has[k], halo1[k].start)

    def induce(src, acc):
        rows = [jnp.broadcast_to(gath[src, r : r + 1, :], (8, LANES)) for r in range(7)]
        sx, sy, sz, dx, dy, dz, gam = rows
        dd = dx * dx + dy * dy + dz * dz
        bias = CORE * dd + CORE * CORE
        gam = gam * (1.0 / FOUR_PI)
        acc = list(acc)
        for g in range(half // 8):
            part = slice(8 * g, 8 * g + 8)
            rx, ry, rz = pb[0, part] - sx, pb[1, part] - sy, pb[2, part] - sz
            along_one = dx * rx + dy * ry + dz * rz
            along_two = along_one - dd
            sq_one = rx * rx + ry * ry + rz * rz + CORE
            sq_two = sq_one - along_one - along_two
            along = along_one * lax.rsqrt(sq_one) - along_two * lax.rsqrt(sq_two)
            kx = dy * rz - dz * ry
            ky = dz * rx - dx * rz
            kz = dx * ry - dy * rx
            w = gam * along / (kx * kx + ky * ky + kz * kz + bias)
            acc[3 * g] += w * kx
            acc[3 * g + 1] += w * ky
            acc[3 * g + 2] += w * kz
        return tuple(acc)

    zero = jnp.zeros((8, LANES), jnp.float32)
    acc = induce(me, (zero,) * (3 * (half // 8)))

    def wake_step(i, acc):
        src = lax.rem(me + n - i, n)
        pltpu.make_async_remote_copy(
            src_ref=gath.at[src],
            dst_ref=gath.at[src],
            send_sem=wake_send.at[i],
            recv_sem=wake_recv.at[src],
            device_id=dev(src),
            device_id_type=MESH,
        ).wait_recv()
        return induce(src, acc)

    acc = lax.fori_loop(1, n, wake_step, acc)
    ax, ay, az = (jnp.concatenate(acc[c::3], axis=0) for c in range(3))
    vel[me, 0:1, :] = jnp.sum(jnp.concatenate([ax, ay], axis=0).T, axis=0, keepdims=True)
    vel[me, 1:2, :] = jnp.sum(jnp.concatenate([az, az], axis=0).T, axis=0, keepdims=True)

    def vel_copy(dst, slot):
        return pltpu.make_async_remote_copy(
            src_ref=vel.at[me],
            dst_ref=vel.at[me],
            send_sem=vel_send.at[slot],
            recv_sem=vel_recv.at[me],
            device_id=dev(dst),
            device_id_type=MESH,
        )

    @pl.loop(1, n)
    def _(i):
        vel_copy(lax.rem(me + i, n), i).start()

    loads[3].wait()
    for k in range(4):
        guarded(arrives[k], halo1[k].wait_recv)

    def second(x, total):
        m = m_v[x]
        for c in range(3):
            u = relaxed(mid_v, 1, c, x, m)
            out_v[c, x] = u
            if c == 1:
                total += circ_v[x] * u
        return total

    profile = lax.fori_loop(0, cx, second, jnp.zeros((cy, cz), jnp.float32))
    store_inner = pltpu.make_async_copy(
        out_v.at[:, pl.ds(2, cx - 3)], out_ref.at[:, pl.ds(2, cx - 3)], sem_out.at[0]
    )
    store_inner.start()

    z_id = lax.broadcasted_iota(jnp.int32, (cz, LANES), 0)

    @pl.loop(0, n_pair)
    def _(q):
        even = jnp.broadcast_to(gath[2 * q, 7:8, :], (8, LANES))
        odd = jnp.broadcast_to(gath[2 * q + 1, 7:8, :], (8, LANES))
        slot = jnp.where(low1, even, odd).astype(jnp.int32)
        owner = pltpu.roll(jnp.where(low1, odd, even), half, 1).astype(jnp.int32)
        row = (slot >> zbits) - j * cy
        col = slot & (cz - 1)
        keys[q, 0] = jnp.where(owner == b, row, -4 * cy * n_bld)
        keys[q, 1] = jnp.where(owner == b + 1, row, -4 * cy * n_bld)
        cols = pl.ds(pl.multiple_of(q * LANES, LANES), LANES)
        zt[:, cols] = jnp.where(z_id == col[0:1, :], 1.0, 0.0).astype(jnp.bfloat16)

    y_id = lax.broadcasted_iota(jnp.int32, (cy, LANES), 0)
    edge_id = jnp.where(y_id >= 6, -2, jnp.where((y_id & 1) == 0, -1, cy))

    def vel_wait(i, carry):
        src = lax.rem(me + n - i, n)
        pltpu.make_async_remote_copy(
            src_ref=vel.at[src],
            dst_ref=vel.at[src],
            send_sem=vel_send.at[i],
            recv_sem=vel_recv.at[src],
            device_id=dev(src),
            device_id_type=MESH,
        ).wait_recv()
        return carry

    lax.fori_loop(1, n, vel_wait, 0)

    n_row = 7 * cy

    @pl.loop(0, n_pair)
    def _(q):
        e0 = jnp.broadcast_to(vel[2 * q, 0:1, :], (8, LANES))
        e1 = jnp.broadcast_to(vel[2 * q, 1:2, :], (8, LANES))
        o0 = jnp.broadcast_to(vel[2 * q + 1, 0:1, :], (8, LANES))
        o1 = jnp.broadcast_to(vel[2 * q + 1, 1:2, :], (8, LANES))
        v = (
            jnp.where(low1, e0, pltpu.roll(o0, half, 1))[0:1],
            jnp.where(low1, pltpu.roll(e0, half, 1), o0)[0:1],
            jnp.where(low1, e1, o1)[0:1],
        )
        key_own = keys[q, 0, 0:1, :]
        key_next = keys[q, 1, 0:1, :]
        own = y_id == key_own
        nxt = y_id == key_next
        edge = edge_id == key_own
        v_edge = jnp.where(y_id < 2, v[0], jnp.where(y_id < 4, v[1], v[2]))
        parts = [jnp.where(own, v[c], 0.0) for c in range(3)]
        parts += [jnp.where(nxt, v[c], 0.0) for c in range(3)]
        parts += [jnp.where(edge, v_edge, 0.0)]
        cols = pl.ds(pl.multiple_of(q * LANES, LANES), LANES)
        for k, part in enumerate(parts):
            high = part.astype(jnp.bfloat16)
            rest = (part - high.astype(jnp.float32)).astype(jnp.bfloat16)
            lhs[k * cy : (k + 1) * cy, cols] = high
            lhs[n_row + k * cy : n_row + (k + 1) * cy, cols] = rest

    dot = lax.dot_general(
        lhs[...], zt[...], (((1,), (1,)), ((), ())), preferred_element_type=jnp.float32
    )
    face = dot[:n_row] + dot[n_row:]

    guarded(has[0], diag_copy.wait_recv)
    m_first, m_second, m_last = m_v[0], m_v[1], m_v[cx - 1]
    m_next = OMEGA / (6.0 + dgn_v[...])
    m_left = OMEGA / (6.0 + yrecv[0, 0, 3, 0:1, :])
    m_right = OMEGA / (6.0 + yrecv[0, 1, 3, 0:1, :])
    for c in (1, 0, 2):
        one = m_first * face[c * cy : (c + 1) * cy]
        one_next = m_next * face[(3 + c) * cy : (4 + c) * cy]
        base = 6 * cy + 2 * c
        left = m_left * face[base : base + 1]
        right = m_right * face[base + 1 : base + 2]
        add_first = (2.0 - OMEGA) * one + m_first * beside_plane(one, left, right)
        add_second = m_second * one
        add_last = m_last * one_next
        if c == 1:
            profile += circ_v[0] * add_first + circ_v[1] * add_second
            profile += circ_v[cx - 1] * add_last
            prof[b] = jnp.broadcast_to(jnp.sum(profile, axis=1, keepdims=True), (cy, LANES))

            def prof_copy(dst, slot):
                return pltpu.make_async_remote_copy(
                    src_ref=prof.at[b],
                    dst_ref=prof.at[b],
                    send_sem=prof_send.at[slot],
                    recv_sem=prof_recv.at[b],
                    device_id=(dst, j),
                    device_id_type=MESH,
                )

            @pl.loop(1, n_blk)
            def _(i):
                prof_copy(lax.rem(b + i, n_blk), i).start()

        out_v[c, 0] += add_first
        out_v[c, 1] += add_second
        out_v[c, cx - 1] += add_last

    store_low = pltpu.make_async_copy(
        out_v.at[:, pl.ds(0, 2)], out_ref.at[:, pl.ds(0, 2)], sem_out.at[1]
    )
    store_high = pltpu.make_async_copy(
        out_v.at[:, pl.ds(cx - 1, 1)], out_ref.at[:, pl.ds(cx - 1, 1)], sem_out.at[2]
    )
    store_low.start()
    store_high.start()

    @pl.loop(1, n)
    def _(i):
        wake_copy(lax.rem(me + i, n), i).wait_send()
        vel_copy(lax.rem(me + i, n), i).wait_send()

    for k in range(4):
        guarded(has[k], halo0[k].wait_send)
        guarded(has[k], halo1[k].wait_send)
    guarded(has[1], diag_copy.wait_send)

    @pl.loop(1, n_blk)
    def _(i):
        src = lax.rem(b + n_blk - i, n_blk)
        pltpu.make_async_remote_copy(
            src_ref=prof.at[src],
            dst_ref=prof.at[src],
            send_sem=prof_send.at[i],
            recv_sem=prof_recv.at[src],
            device_id=(src, j),
            device_id_type=MESH,
        ).wait_recv()

    table = prof[...].reshape(n_blk * cy, LANES)
    spot = lax.broadcasted_iota(jnp.int32, (n_blk * cy, LANES), 0) == seg_place.astype(jnp.int32)
    looked = jnp.sum(jnp.where(spot, table, 0.0), axis=0, keepdims=True)
    ng_ref[...] = (1.0 - RELAX) * gam_ref[...] + RELAX * looked

    @pl.loop(1, n_blk)
    def _(i):
        prof_copy(lax.rem(b + i, n_blk), i).wait_send()

    store_inner.wait()
    store_low.wait()
    store_high.wait()


def per_device(
    n_blk,
    n_bld,
    bnd_pos,
    bnd_owner,
    bnd_slot,
    seg_start,
    seg_step,
    seg_gamma,
    seg_sec,
    flow,
    source,
    extra_diag,
    circ_weight,
    sec_block,
    sec_row,
):
    n = n_blk * n_bld
    _, cx, cy, cz = flow.shape
    cells = bnd_pos.shape[1]
    half = cells // n_bld
    n_cells = n * half
    f32 = jnp.float32
    vmem = pl.BlockSpec(memory_space=pltpu.VMEM)
    hbm = pl.BlockSpec(memory_space=pl.ANY)
    dma = pltpu.SemaphoreType.DMA
    return pl.pallas_call(
        functools.partial(kernel, n_blk, n_bld),
        out_shape=(
            jax.ShapeDtypeStruct(flow.shape, f32),
            jax.ShapeDtypeStruct(seg_gamma.shape, f32),
        ),
        in_specs=[vmem] * 9 + [hbm] * 4,
        out_specs=(hbm, vmem),
        scratch_shapes=[
            pltpu.VMEM((n, 8, LANES), f32),
            pltpu.VMEM((n, 2, LANES), f32),
            pltpu.VMEM((n_blk, cy, LANES), f32),
            pltpu.VMEM((3, cx + 2, cy, cz), f32),
            pltpu.VMEM((3, cx + 2, cy, cz), f32),
            pltpu.VMEM((3, cx, cy, cz), f32),
            pltpu.VMEM((3, cx, cy, cz), f32),
            pltpu.VMEM((cx, cy, cz), f32),
            pltpu.VMEM((cx, cy, cz), f32),
            pltpu.VMEM((cx, cy, cz), f32),
            pltpu.VMEM((2, 2, 4, cx, cz), f32),
            pltpu.VMEM((2, 2, 4, cx, cz), f32),
            pltpu.VMEM((cy, cz), f32),
            pltpu.VMEM((8, cells), f32),
            pltpu.VMEM((cells, 8), f32),
            pltpu.VMEM((3, half, LANES), f32),
            pltpu.VMEM((n // 2, 2, 8, LANES), jnp.int32),
            pltpu.VMEM((cz, n_cells), jnp.bfloat16),
            pltpu.VMEM((14 * cy, n_cells), jnp.bfloat16),
            dma((4,)),
            dma((3,)),
            dma((n,)),
            dma((n,)),
            dma((n,)),
            dma((n,)),
            dma((n_blk,)),
            dma((n_blk,)),
            dma((9,)),
            dma((9,)),
        ],
        compiler_params=pltpu.CompilerParams(
            collective_id=0, has_side_effects=True, vmem_limit_bytes=40 * 1024 * 1024
        ),
    )(
        bnd_pos,
        bnd_owner.reshape(cells // LANES, LANES),
        bnd_slot.reshape(cells // LANES, LANES),
        seg_start,
        seg_step,
        seg_gamma,
        seg_sec,
        sec_block,
        sec_row,
        flow,
        source,
        extra_diag,
        circ_weight,
    )


def solution(mesh):
    return jax.shard_map(
        functools.partial(per_device, mesh.shape["blk"], mesh.shape["blade"]),
        mesh=mesh,
        in_specs=(
            P(None, "blk"),
            P("blk", None),
            P("blk"),
            P(None, "blade", "blk"),
            P(None, "blade", "blk"),
            P("blade", "blk"),
            P("blade", "blk"),
            P(None, "blk", "blade", None),
            P(None, "blk", "blade", None),
            P("blk", "blade", None),
            P("blk", "blade", None),
            P(),
            P(),
        ),
        out_specs=(P(None, "blk", "blade", None), P("blade", "blk")),
        check_vma=False,
    )
```

time: 137 us -> 39.5 us (0.29); the launches traced: 135 us -> 39.1 us
  blocking collectives: 61.7 us -> 0 us
  other arithmetic: 35.1 us -> 0 us
  Pallas kernels: 0 us -> 27.9 us
  starting transfers between devices: 25.3 us -> 0 us
  waiting for transfers between devices: 3.77 us -> 0 us
  local copies, waits for them, and re-layouts: 7.59 us -> 10.5 us
    all_gather x1 -> x0, blocking collectives: 32.2 us -> none  [per_device(): lax.all_gather(own_wake, 'blk', axis=1, tiled=True)]
    pallas_call x0 -> x1, Pallas kernels: none -> 27.9 us  [per_device(): pl.pallas_call(functools.partial(kernel, n_blk, n_bld), out_shape=(jax.Sh...]
    scatter-add x2 -> x0, other arithmetic: 24.6 us -> none  [the longest x1 24.6 us: per_device(): face = jnp.zeros((3, depth_y, depth_z), jnp.float32).at[:, jnp.clip(local...]
    unnamed x1 -> x0, blocking collectives: 23.8 us -> none
    ppermute x8 -> x0, starting transfers between devices: 19.8 us -> none  [the longest x4 14.7 us: with_halo(): before = lax.ppermute(last, axis, up)]
    unnamed x30 -> x28, local copies, waits for them, and re-layouts: 3.29 us -> 10.5 us
    psum x1 -> x0, blocking collectives: 5.67 us -> none  [per_device(): velocity = lax.psum(partial_value, 'blade')]
    all_to_all x1 -> x0, starting transfers between devices: 5.46 us -> none  [per_device(): lax.all_to_all(outgoing, 'blk', split_axis=1, concat_axis=1, tiled=True)]
  transfers between devices with their start and end apart: 9 -> 0, of which waited for: 4 -> 0; matrix products, arithmetic and copies ran while one was open for 21% -> 0% of each run, Pallas kernels for 0% -> 0%
where the time goes in v1:
time: 39.5 us; the launch traced here: 39.1 us
  Pallas kernels  27.9 us (71%)
  local copies, waits for them, and re-layouts  10.5 us (27%)
  between operations  0.67 us (2%)
    pallas_call x1, Pallas kernels, per_device(): pl.pallas_call(functools.partial(kernel, n_blk, n_bld), out_shape=(jax.Sh...  27.9 us
    unnamed x28, local copies, waits for them, and re-layouts  10.5 us

profile of v1, /device:TPU:0, one launch (start us, length us, event | category | flops | bytes accessed | tf_op | source)
XLA Modules:
  0.0 39.1 jit_solution(16937802933576243591)
XLA Ops:
  0.6 0.0 copy-start.5
  0.6 0.0 copy-start.7
  0.7 0.7 %copy-done.5 = s32[4,64]{1,0:T(4,128)S(1)} copy-done((s32[4,64]{1,0:T(4,128)S(1)}, s32[4,64]{1,0:T(4,128)}, u32[]{:S(2)}) %copy-start.5) | copy-done | bytes 1048
  1.3 0.0 copy-done.7
  1.3 0.0 copy-start
  1.3 1.0 %copy-done = f32[3,8,16,256]{3,2,1,0:T(8,128)S(1)} copy-done((f32[3,8,16,256]{3,2,1,0:T(8,128)S(1)}, f32[3,8,16,256]{3,2,1,0:T(8,128)}, u32[]{:S(2)}) %copy-start) | copy-done | bytes 393240
  2.3 0.0 copy-start.1
  2.3 1.0 %copy-done.1 = f32[3,8,16,256]{3,2,1,0:T(8,128)S(1)} copy-done((f32[3,8,16,256]{3,2,1,0:T(8,128)S(1)}, f32[3,8,16,256]{3,2,1,0:T(8,128)}, u32[]{:S(2)}) %copy-start.1) | copy-done | bytes 393240
  3.3 0.0 copy-start.2
  3.3 0.9 %copy-done.2 = f32[8,16,256]{2,1,0:T(8,128)S(1)} copy-done((f32[8,16,256]{2,1,0:T(8,128)S(1)}, f32[8,16,256]{2,1,0:T(8,128)}, u32[]{:S(2)}) %copy-start.2) | copy-done | bytes 131096
  4.2 0.0 copy-start.3
  4.2 0.9 %copy-done.3 = f32[8,16,256]{2,1,0:T(8,128)S(1)} copy-done((f32[8,16,256]{2,1,0:T(8,128)S(1)}, f32[8,16,256]{2,1,0:T(8,128)}, u32[]{:S(2)}) %copy-start.3) | copy-done | bytes 131096
  5.1 0.0 copy-start.4
  5.1 0.7 %copy-done.4 = f32[3,256]{1,0:T(4,128)S(1)} copy-done((f32[3,256]{1,0:T(4,128)S(1)}, f32[3,256]{1,0:T(4,128)}, u32[]{:S(2)}) %copy-start.4) | copy-done | bytes 3096
  5.8 0.0 copy-start.6
  5.8 0.7 %copy-done.6 = s32[4,64]{1,0:T(4,128)S(1)} copy-done((s32[4,64]{1,0:T(4,128)S(1)}, s32[4,64]{1,0:T(4,128)}, u32[]{:S(2)}) %copy-start.6) | copy-done | bytes 1048
  6.5 0.7 %copy-done.8 = f32[3,1,128]{2,1,0:T(1,128)S(1)} copy-done((f32[3,1,128]{2,1,0:T(1,128)S(1)}, f32[3,1,128]{2,1,0:T(1,128)}, u32[]{:S(2)}) %copy-start.8) | copy-done | bytes 1560
  7.2 0.7 %copy-done.9 = s32[256,1]{0,1:T(1,128)S(1)} copy-done((s32[256,1]{0,1:T(1,128)S(1)}, s32[256,1]{0,1:T(1,128)}, u32[]{:S(2)}) %copy-start.9) | copy-done | bytes 1048
  7.9 0.7 %copy-done.10 = s32[256]{0:T(256)S(1)} copy-done((s32[256]{0:T(256)S(1)}, s32[256]{0:T(256)}, u32[]{:S(2)}) %copy-start.10) | copy-done | bytes 1048
  8.5 0.7 %copy-done.11 = f32[1,128]{1,0:T(1,128)S(1)} copy-done((f32[1,128]{1,0:T(1,128)S(1)}, f32[1,128]{1,0:T(1,128)}, u32[]{:S(2)}) %copy-start.11) | copy-done | bytes 536
  9.2 0.7 %copy-done.12 = s32[1,128]{1,0:T(1,128)S(1)} copy-done((s32[1,128]{1,0:T(1,128)S(1)}, s32[1,128]{1,0:T(1,128)}, u32[]{:S(2)}) %copy-start.12) | copy-done | bytes 536
  9.9 27.9 %shard_map.140 = (f32[3,8,16,256]{3,2,1,0:T(8,128)S(1)}, f32[1,128]{1,0:T(1,128)S(1)}) custom-call(f32[3,256]{1,0:T(4,128)S(1)} %copy-done.4, s32[2,128]{1,0:T(2,128)S(1)} %bitcast.2, s32[2,128]{1,0:T(2,128)S(1)} %bitcast.3, f32[3,1,128]{2,1,0:T(1,128)S(1)} %copy-done.7, f32[3,1,128]{2,1,0:T(1,128)S(1)} %copy-done.8, f32[1,128]{1,0:T(1,128)S(1)} %copy-done.11, ...), custom_call_target="tpu_custom_call" | custom-call | tf_op jit(solution)/shard_map/pallas_call | solution.py:511
  37.8 0.7 %copy.17 = f32[3,8,16,256]{3,2,1,0:T(8,128)} copy(f32[3,8,16,256]{3,2,1,0:T(8,128)S(1)} %get-tuple-element.4) | data formatting | bytes 786432
  38.6 0.5 %copy.18 = f32[1,128]{1,0:T(1,128)} copy(f32[1,128]{1,0:T(1,128)S(1)} %get-tuple-element.5) | data formatting | bytes 1024
  (5 shorter events, 0.0 us)
Async XLA Ops:
  0.6 0.7 %copy-start.5 = (s32[4,64]{1,0:T(4,128)S(1)}, s32[4,64]{1,0:T(4,128)}, u32[]{:S(2)}) copy-start(s32[4,64]{1,0:T(4,128)} %sblk_ref.1) | copy-start | bytes 3076
  0.6 0.7 %copy-start.7 = (f32[3,1,128]{2,1,0:T(1,128)S(1)}, f32[3,1,128]{2,1,0:T(1,128)}, u32[]{:S(2)}) copy-start(f32[3,1,128]{2,1,0:T(1,128)} %start_ref.1) | copy-start | bytes 4612
  1.3 1.0 %copy-start = (f32[3,8,16,256]{3,2,1,0:T(8,128)S(1)}, f32[3,8,16,256]{3,2,1,0:T(8,128)}, u32[]{:S(2)}) copy-start(f32[3,8,16,256]{3,2,1,0:T(8,128)} %flow_ref.1) | copy-start | bytes 1179652
  2.3 1.0 %copy-start.1 = (f32[3,8,16,256]{3,2,1,0:T(8,128)S(1)}, f32[3,8,16,256]{3,2,1,0:T(8,128)}, u32[]{:S(2)}) copy-start(f32[3,8,16,256]{3,2,1,0:T(8,128)} %src_ref.1) | copy-start | bytes 1179652
  3.3 0.9 %copy-start.2 = (f32[8,16,256]{2,1,0:T(8,128)S(1)}, f32[8,16,256]{2,1,0:T(8,128)}, u32[]{:S(2)}) copy-start(f32[8,16,256]{2,1,0:T(8,128)} %diag_ref.1) | copy-start | bytes 393220
  4.2 0.9 %copy-start.3 = (f32[8,16,256]{2,1,0:T(8,128)S(1)}, f32[8,16,256]{2,1,0:T(8,128)}, u32[]{:S(2)}) copy-start(f32[8,16,256]{2,1,0:T(8,128)} %circ_ref.1) | copy-start | bytes 393220
  5.1 0.7 %copy-start.4 = (f32[3,256]{1,0:T(4,128)S(1)}, f32[3,256]{1,0:T(4,128)}, u32[]{:S(2)}) copy-start(f32[3,256]{1,0:T(4,128)} %pos_ref.1) | copy-start | bytes 9220
  5.8 0.7 %copy-start.6 = (s32[4,64]{1,0:T(4,128)S(1)}, s32[4,64]{1,0:T(4,128)}, u32[]{:S(2)}) copy-start(s32[4,64]{1,0:T(4,128)} %srow_ref.1) | copy-start | bytes 3076
  6.5 0.7 %copy-start.8 = (f32[3,1,128]{2,1,0:T(1,128)S(1)}, f32[3,1,128]{2,1,0:T(1,128)}, u32[]{:S(2)}) copy-start(f32[3,1,128]{2,1,0:T(1,128)} %step_ref.1) | copy-start | bytes 4612
  7.2 0.7 %copy-start.9 = (s32[256,1]{0,1:T(1,128)S(1)}, s32[256,1]{0,1:T(1,128)}, u32[]{:S(2)}) copy-start(s32[256,1]{0,1:T(1,128)} %param.14) | copy-start | bytes 3076
  7.9 0.7 %copy-start.10 = (s32[256]{0:T(256)S(1)}, s32[256]{0:T(256)}, u32[]{:S(2)}) copy-start(s32[256]{0:T(256)} %param.15) | copy-start | bytes 3076
  8.5 0.7 %copy-start.11 = (f32[1,128]{1,0:T(1,128)S(1)}, f32[1,128]{1,0:T(1,128)}, u32[]{:S(2)}) copy-start(f32[1,128]{1,0:T(1,128)} %gam_ref.1) | copy-start | bytes 1540
  9.2 0.7 %copy-start.12 = (s32[1,128]{1,0:T(1,128)S(1)}, s32[1,128]{1,0:T(1,128)}, u32[]{:S(2)}) copy-start(s32[1,128]{1,0:T(1,128)} %sec_ref.1) | copy-start | bytes 1540

commit v2 on v1

--- a/solution.py
+++ b/solution.py
@@ -19,6 +19,21 @@
 def kernel(
     n_blk,
     n_bld,
+    pos_hbm,
+    own_hbm,
+    slot_hbm,
+    start_hbm,
+    step_hbm,
+    gam_hbm,
+    sec_hbm,
+    sblk_hbm,
+    srow_hbm,
+    flow_ref,
+    src_ref,
+    diag_ref,
+    circ_ref,
+    out_ref,
+    ng_hbm,
     pos_ref,
     own_ref,
     slot_ref,
@@ -28,11 +43,6 @@
     sec_ref,
     sblk_ref,
     srow_ref,
-    flow_ref,
-    src_ref,
-    diag_ref,
-    circ_ref,
-    out_ref,
     ng_ref,
     gath,
     vel,
@@ -76,6 +86,24 @@
     def dev(d):
         return (lax.div(d, n_bld), lax.rem(d, n_bld))
 
+    small = [
+        pltpu.make_async_copy(source, target, sem_in.at[4 + k])
+        for k, (source, target) in enumerate(
+            (
+                (start_hbm, start_ref),
+                (step_hbm, step_ref),
+                (gam_hbm, gam_ref),
+                (slot_hbm, slot_ref),
+                (own_hbm, own_ref),
+                (pos_hbm, pos_ref),
+                (sec_hbm, sec_ref),
+                (sblk_hbm, sblk_ref),
+                (srow_hbm, srow_ref),
+            )
+        )
+    ]
+    for copy in small:
+        copy.start()
     loads = [
         pltpu.make_async_copy(flow_ref, flow_v.at[:, pl.ds(1, cx)], sem_in.at[0]),
         pltpu.make_async_copy(diag_ref, diag_v, sem_in.at[1]),
@@ -92,6 +120,9 @@
         pl.semaphore_signal(
             barrier, inc=1, device_id=dev(lax.rem(me + i, n)), device_id_type=MESH
         )
+
+    for copy in small:
+        copy.wait()
 
     lane1 = lax.broadcasted_iota(jnp.int32, (8, LANES), 1)
     low1 = lane1 < half
@@ -237,25 +268,6 @@
         right = yrecv[stage, 1, c, pl.ds(x, 1), :]
         beside = beside_plane(u, left, right) + grid[c, x] + grid[c, x + 2]
         return (1.0 - OMEGA) * u + m * (src_v[c, x] + beside)
-
-    loads[2].wait()
-    for k in range(4):
-        guarded(arrives[k], halo0[k].wait_recv)
-
-    @pl.loop(0, cx)
-    def _(x):
-        m = OMEGA / (6.0 + diag_v[x])
-        m_v[x] = m
-        for c in range(3):
-            mid_v[c, x + 1] = relaxed(flow_v, 0, c, x, m)
-
-    for c in range(3):
-        ysend[1, 0, c] = mid_v[c, 1 : cx + 1, cy - 1, :]
-        ysend[1, 1, c] = mid_v[c, 1 : cx + 1, 0, :]
-    ysend[1, 0, 3] = jnp.zeros((cx, cz), jnp.float32)
-    ysend[1, 1, 3] = jnp.zeros((cx, cz), jnp.float32)
-    for k in range(4):
-        guarded(has[k], halo1[k].start)
 
     def induce(src, acc):
         rows = [jnp.broadcast_to(gath[src, r : r + 1, :], (8, LANES)) for r in range(7)]
@@ -296,7 +308,29 @@
         ).wait_recv()
         return induce(src, acc)
 
-    acc = lax.fori_loop(1, n, wake_step, acc)
+    middle = n // 2
+    acc = lax.fori_loop(1, middle, wake_step, acc)
+
+    loads[2].wait()
+    for k in range(4):
+        guarded(arrives[k], halo0[k].wait_recv)
+
+    @pl.loop(0, cx)
+    def _(x):
+        m = OMEGA / (6.0 + diag_v[x])
+        m_v[x] = m
+        for c in range(3):
+            mid_v[c, x + 1] = relaxed(flow_v, 0, c, x, m)
+
+    for c in range(3):
+        ysend[1, 0, c] = mid_v[c, 1 : cx + 1, cy - 1, :]
+        ysend[1, 1, c] = mid_v[c, 1 : cx + 1, 0, :]
+    ysend[1, 0, 3] = jnp.zeros((cx, cz), jnp.float32)
+    ysend[1, 1, 3] = jnp.zeros((cx, cz), jnp.float32)
+    for k in range(4):
+        guarded(has[k], halo1[k].start)
+
+    acc = lax.fori_loop(middle, n, wake_step, acc)
     ax, ay, az = (jnp.concatenate(acc[c::3], axis=0) for c in range(3))
     vel[me, 0:1, :] = jnp.sum(jnp.concatenate([ax, ay], axis=0).T, axis=0, keepdims=True)
     vel[me, 1:2, :] = jnp.sum(jnp.concatenate([az, az], axis=0).T, axis=0, keepdims=True)
@@ -336,7 +370,7 @@
 
     z_id = lax.broadcasted_iota(jnp.int32, (cz, LANES), 0)
 
-    @pl.loop(0, n_pair)
+    @pl.loop(0, n_pair, unroll=4)
     def _(q):
         even = jnp.broadcast_to(gath[2 * q, 7:8, :], (8, LANES))
         odd = jnp.broadcast_to(gath[2 * q + 1, 7:8, :], (8, LANES))
@@ -368,7 +402,7 @@
 
     n_row = 7 * cy
 
-    @pl.loop(0, n_pair)
+    @pl.loop(0, n_pair, unroll=4)
     def _(q):
         e0 = jnp.broadcast_to(vel[2 * q, 0:1, :], (8, LANES))
         e1 = jnp.broadcast_to(vel[2 * q, 1:2, :], (8, LANES))
@@ -417,7 +451,9 @@
         if c == 1:
             profile += circ_v[0] * add_first + circ_v[1] * add_second
             profile += circ_v[cx - 1] * add_last
-            prof[b] = jnp.broadcast_to(jnp.sum(profile, axis=1, keepdims=True), (cy, LANES))
+            folded = sum(profile[:, k : k + LANES] for k in range(0, cz, LANES))
+            folded = jnp.concatenate([folded, jnp.zeros((LANES - cy, LANES), jnp.float32)], axis=0)
+            prof[b] = jnp.sum(folded.T, axis=0, keepdims=True)
 
             def prof_copy(dst, slot):
                 return pltpu.make_async_remote_copy(
@@ -468,10 +504,15 @@
             device_id_type=MESH,
         ).wait_recv()
 
-    table = prof[...].reshape(n_blk * cy, LANES)
-    spot = lax.broadcasted_iota(jnp.int32, (n_blk * cy, LANES), 0) == seg_place.astype(jnp.int32)
-    looked = jnp.sum(jnp.where(spot, table, 0.0), axis=0, keepdims=True)
+    table = prof[:, 0, :].T
+    place_id = seg_place.astype(jnp.int32)
+    looked = jnp.zeros((cy, LANES), jnp.float32)
+    for k in range(n_blk):
+        looked += jnp.where(y_id + k * cy == place_id, table[:cy, k : k + 1], 0.0)
+    looked = jnp.sum(looked, axis=0, keepdims=True)
     ng_ref[...] = (1.0 - RELAX) * gam_ref[...] + RELAX * looked
+    store_ng = pltpu.make_async_copy(ng_ref, ng_hbm, sem_out.at[3])
+    store_ng.start()
 
     @pl.loop(1, n_blk)
     def _(i):
@@ -480,6 +521,7 @@
     store_inner.wait()
     store_low.wait()
     store_high.wait()
+    store_ng.wait()
 
 
 def per_device(
@@ -505,8 +547,7 @@
     half = cells // n_bld
     n_cells = n * half
     f32 = jnp.float32
-    vmem = pl.BlockSpec(memory_space=pltpu.VMEM)
-    hbm = pl.BlockSpec(memory_space=pl.ANY)
+    hbm = pl.BlockSpec(memory_space=pltpu.HBM)
     dma = pltpu.SemaphoreType.DMA
     return pl.pallas_call(
         functools.partial(kernel, n_blk, n_bld),
@@ -514,12 +555,22 @@
             jax.ShapeDtypeStruct(flow.shape, f32),
             jax.ShapeDtypeStruct(seg_gamma.shape, f32),
         ),
-        in_specs=[vmem] * 9 + [hbm] * 4,
-        out_specs=(hbm, vmem),
+        in_specs=[hbm] * 13,
+        out_specs=(hbm, hbm),
         scratch_shapes=[
+            pltpu.VMEM(bnd_pos.shape, f32),
+            pltpu.VMEM((cells // LANES, LANES), jnp.int32),
+            pltpu.VMEM((cells // LANES, LANES), jnp.int32),
+            pltpu.VMEM(seg_start.shape, f32),
+            pltpu.VMEM(seg_step.shape, f32),
+            pltpu.VMEM(seg_gamma.shape, f32),
+            pltpu.VMEM(seg_sec.shape, jnp.int32),
+            pltpu.VMEM(sec_block.shape, jnp.int32),
+            pltpu.VMEM(sec_row.shape, jnp.int32),
+            pltpu.VMEM(seg_gamma.shape, f32),
             pltpu.VMEM((n, 8, LANES), f32),
             pltpu.VMEM((n, 2, LANES), f32),
-            pltpu.VMEM((n_blk, cy, LANES), f32),
+            pltpu.VMEM((n_blk, 1, LANES), f32),
             pltpu.VMEM((3, cx + 2, cy, cz), f32),
             pltpu.VMEM((3, cx + 2, cy, cz), f32),
             pltpu.VMEM((3, cx, cy, cz), f32),
@@ -536,8 +587,8 @@
             pltpu.VMEM((n // 2, 2, 8, LANES), jnp.int32),
             pltpu.VMEM((cz, n_cells), jnp.bfloat16),
             pltpu.VMEM((14 * cy, n_cells), jnp.bfloat16),
+            dma((13,)),
             dma((4,)),
-            dma((3,)),
             dma((n,)),
             dma((n,)),
             dma((n,)),
@@ -548,7 +599,7 @@
             dma((9,)),
         ],
         compiler_params=pltpu.CompilerParams(
-            collective_id=0, has_side_effects=True, vmem_limit_bytes=40 * 1024 * 1024
+            collective_id=0, has_side_effects=True, vmem_limit_bytes=56 * 1024 * 1024
         ),
     )(
         bnd_pos,

time: 39.5 us -> 29.4 us (0.74)
  local copies, waits for them, and re-layouts: 10.5 us -> 2.28 us
  Pallas kernels: 27.9 us -> 26.3 us
    unnamed x28 -> x4, local copies, waits for them, and re-layouts: 10.5 us -> 2.28 us
    pallas_call x1, Pallas kernels: 27.9 us -> 26.3 us  [per_device(): pl.pallas_call(functools.partial(kernel, n_blk, n_bld), out_shape=(jax.Sh...]
where the time goes in v2:
time: 29.4 us; the launch traced here: 29.2 us
  Pallas kernels  26.3 us (89%)
  local copies, waits for them, and re-layouts  2.28 us (8%)
  between operations  0.65 us (2%)
    pallas_call x1, Pallas kernels, per_device(): pl.pallas_call(functools.partial(kernel, n_blk, n_bld), out_shape=(jax.Sh...  26.3 us
    unnamed x4, local copies, waits for them, and re-layouts  2.28 us

profile of v2, /device:TPU:0, one launch (start us, length us, event | category | flops | bytes accessed | tf_op | source)
XLA Modules:
  0.0 29.2 jit_solution(3133768641334447294)
XLA Ops:
  0.6 26.3 %shard_map.140 = (f32[3,8,16,256]{3,2,1,0:T(8,128)}, f32[1,128]{1,0:T(1,128)}) custom-call(f32[3,256]{1,0:T(4,128)} %pos_hbm.1, s32[2,128]{1,0:T(2,128)} %bitcast.2, s32[2,128]{1,0:T(2,128)} %bitcast.3, f32[3,1,128]{2,1,0:T(1,128)} %start_hbm.1, f32[3,1,128]{2,1,0:T(1,128)} %step_hbm.1, f32[1,128]{1,0:T(1,128)} %gam_hbm.1, s32[1,128]{1,0:T(1,128)} %sec_hbm.1, ...), custom_call_target="tpu_custom_call" | custom-call | tf_op jit(solution)/shard_map/pallas_call | solution.py:552
  26.9 0.0 copy-start
  27.0 1.8 %copy.17 = f32[3,8,16,256]{3,2,1,0:T(8,128)} copy(f32[3,8,16,256]{3,2,1,0:T(8,128)} %get-tuple-element.4) | data formatting | bytes 786432
  28.7 0.0 copy-done
  28.7 0.5 %copy.18 = f32[1,128]{1,0:T(1,128)} copy(f32[1,128]{1,0:T(1,128)S(1)} %copy-done) | data formatting | bytes 1024
Async XLA Ops:
  26.9 1.8 %copy-start = (f32[1,128]{1,0:T(1,128)S(1)}, f32[1,128]{1,0:T(1,128)}, u32[]{:S(2)}) copy-start(f32[1,128]{1,0:T(1,128)} %get-tuple-element.5) | copy-start | bytes 1540
